TPU v7x, 32 devices: a whole 2x2x4 slice. The times are simulated.
32 devices in a mesh: layer: 2 (over x), row: 16 (over z, y, core).
Axes of the slice: x: 2, y: 2, z: 4, core: 2. Of those that a mesh axis runs over, the one named last changes fastest.
Arguments:
- deltas: bfloat16 [2, 2, 1024, 16384], P('layer', None, 'row'), parts along dimension 0, may hold values from -6 to 6
- basis: bfloat16 [16384, 128], P('row'), may hold values from -0.046875 to 0.046875
Outputs:
- merged: bfloat16 [2, 1024, 16384], P('layer', None, 'row'), parts along dimension 0
There are 2 independent parts, one for each index of `layer`. A program takes and returns all parts, laid end to end along the dimension named above; an argument that names none is the same for every part. Nothing has to cross between parts.
All inputs are finite; a program needn't handle non-finite values.
Results may differ from a plain program's by a relative error of at most 0.0081.
Values may be sent and summed in bfloat16 or wider, within the bound.
A program may use at most 64 MiB of HBM per device.

v0:
```python
import jax
import jax.numpy as jnp
from jax import lax
from jax.sharding import PartitionSpec as P


def whiten_rows(factors, chol_factor):
    return lax.linalg.triangular_solve(
        chol_factor, factors.astype(jnp.float32), left_side=False, lower=True, transpose_a=True
    ).astype(jnp.bfloat16)


def inner_rows(left, right):
    return lax.dot_general(
        left, right, (((0,), (0,)), ((), ())), preferred_element_type=jnp.float32
    )


def shards(deltas, basis):
    group_deltas = deltas[0]
    task_count, rows_local, col_count = group_deltas.shape
    rank_width = basis.shape[1]
    factor_width = task_count * rank_width
    sketch = jnp.einsum(
        "trc,ck->trk",
        group_deltas,
        lax.all_gather(basis, "row", axis=0, tiled=True),
        preferred_element_type=jnp.float32,
    )
    factors = sketch.astype(jnp.bfloat16).transpose(1, 0, 2).reshape(rows_local, factor_width)
    gram_sum = lax.psum(inner_rows(factors, factors), "row")
    chol_factor = jnp.linalg.cholesky(gram_sum)
    local_white = whiten_rows(factors, chol_factor)
    whitened = lax.all_gather(local_white, "row", axis=0, tiled=True)
    task_sum = jnp.sum(group_deltas.astype(jnp.float32), axis=0).astype(jnp.bfloat16)
    columns = lax.all_to_all(task_sum, "row", split_axis=1, concat_axis=0, tiled=True)
    coeffs = inner_rows(columns, whitened).astype(jnp.bfloat16)
    merged = lax.dot_general(
        whitened, coeffs, (((1,), (1,)), ((), ())), preferred_element_type=jnp.float32
    )
    return merged.astype(jnp.bfloat16)[None]


def solution(mesh):
    return jax.shard_map(
        shards,
        mesh=mesh,
        in_specs=(P("layer", None, "row", None), P("row", None)),
        out_specs=P("layer", None, "row"),
        check_vma=False,
    )
```

profile of v0, /device:TPU:0, one launch (start us, length us, event | category | flops | bytes accessed | tf_op | source)
XLA Modules:
  0.0 280.6 jit_solution(7670902479510973924)
XLA Ops:
  6.5 0.7 all-gather.2.cloned.1.call-update
  7.3 3.2 %reduce_sum.12 = bf16[64,16384]{1,0:T(8,128)(2,1)S(1)} reduce(bf16[1,2,64,16384]{3,2,1,0:T(8,128)(2,1)} %param.2, bf16[]{:T(256)} %constant.79.clone.1), dimensions={0,1}, to_apply=%region_5.6 | reduce | flops 1048576 | bytes 6291458 | tf_op jit(solution)/shard_map/reduce_sum | solution.py:35
  10.5 1.6 copy.22
  12.1 7.4 %all-to-all-start = ((bf16[64,16,1024]{2,0,1:T(8,128)(2,1)}), bf16[64,16,1024]{2,0,1:T(8,128)(2,1)S(1)}, u32[]{:S(2)}, u32[]{:S(2)}) async-start(bf16[64,16,1024]{2,0,1:T(8,128)(2,1)} %bitcast.67), calls=%async_computation | async-start | bytes 4194304 | tf_op jit(solution)/shard_map/all_to_all | solution.py:36
  19.5 67.8 %all-gather.2.cloned.1.call-done = bf16[16384,128]{1,0:T(8,128)(2,1)} async-done(((bf16[1024,128]{1,0:T(8,128)(2,1)}), bf16[16384,128]{1,0:T(8,128)(2,1)}) %all-gather.2.cloned.1.call-update) | async-done | bytes 4194320 | tf_op jit(solution)/shard_map/all_gather | solution.py:27
  87.3 4.7 %fusion.8 = bf16[2,8,8,128]{3,2,1,0:T(8,128)(2,1)S(1)} fusion(bf16[16384,128]{1,0:T(8,128)(2,1)} %all-gather.2.cloned.1.call-done, bf16[1,2,64,16384]{3,2,1,0:T(8,128)(2,1)} %param.2), kind=kOutput, calls=%fused_computation.10 | convolution fusion | flops 536887296 | bytes 8421376 | tf_op jit(solution)/shard_map/trc,ck->trk/dot_general | solution.py:24
  92.0 0.9 fusion.20
  93.0 92.4 %all-reduce.3.cloned.1.call-done = f32[256,256]{0,1:T(8,128)} async-done(((f32[256,256]{0,1:T(8,128)}), f32[256,256]{0,1:T(8,128)}) %all-reduce.3.cloned.1.call-update) | async-done | bytes 262160 | tf_op jit(solution)/shard_map/psum | solution.py:31
  185.4 1.1 copy.14
  186.5 1.0 fusion.13
  187.5 11.7 %cholesky.50 = f32[128,128]{1,0:T(8,128)S(1)} custom-call(f32[128,128]{1,0:T(8,128)S(1)} %cholesky.118), custom_call_target="Cholesky" | custom-call | tf_op jit(solution)/shard_map/jit(cholesky)/cholesky | solution.py:32
  199.2 9.8 %custom-call.14 = f32[1,128,128]{1,2,0:T(8,128)S(1)} custom-call(f32[1,128,128]{2,1,0:T(8,128)S(1)} %get-tuple-element.26), custom_call_target="InvertDiagBlocksLowerTriangular" | custom-call | tf_op jit(solution)/shard_map/jit(cholesky)/cholesky | solution.py:32
  209.3 0.3 convolution_subtract_fusion
  209.6 11.7 %cholesky.105 = f32[128,128]{1,0:T(8,128)S(1)} custom-call(f32[128,128]{1,0:T(8,128)S(1)} %convolution_subtract_fusion), custom_call_target="Cholesky" | custom-call | tf_op jit(solution)/shard_map/jit(cholesky)/cholesky | solution.py:32
  221.3 0.7 compare_reduce_fusion
  223.4 4.2 %while.1 = (s32[]{:T(128)}, f32[256,256]{1,0:T(8,128)S(1)}, s32[2,2]{1,0:T(2,128)S(1)}, f32[2,128,128]{2,1,0:T(8,128)S(1)}, s32[]{:T(128)}) while((s32[]{:T(128)}, f32[256,256]{1,0:T(8,128)S(1)}, s32[2,2]{1,0:T(2,128)S(1)}, f32[2,128,128]{2,1,0:T(8,128)S(1)}, s32[]{:T(128)}) %tuple.24), condition=%wide.while_cond, body=%wide.while_body.sunk | while | flops 2 | bytes 131189 | solution.py:8
  223.5 0.7 fusion.31
  224.2 1.3 bitcast_dynamic-update-slice_fusion.2
  225.6 0.7 fusion.31
  226.2 1.3 bitcast_dynamic-update-slice_fusion.2
  227.6 19.7 %custom-call.15 = f32[2,128,128]{1,2,0:T(8,128)S(1)} custom-call(f32[2,128,128]{2,1,0:T(8,128)S(1)} %get-tuple-element.12), custom_call_target="InvertDiagBlocksLowerTriangular" | custom-call | tf_op jit(solution)/shard_map/triangular_solve | solution.py:8
  247.4 0.2 convolution_subtract_fusion.1
  247.9 22.3 %all_gather.7 = bf16[1024,256]{1,0:T(8,128)(2,1)S(1)} all-gather(bf16[64,256]{1,0:T(8,128)(2,1)S(1)} %pad_maximum_fusion), channel_id=1, replica_groups=mesh['layer'=2,'row'=16] {'row'}, dimensions={0}, use_global_device_ids=true | all-gather | bytes 557056 | tf_op jit(solution)/shard_map/all_gather | solution.py:34
  270.2 3.6 %convert_bitcast_fusion = bf16[1,1024,1024]{2,1,0:T(8,128)(2,1)} fusion(bf16[1024,256]{1,0:T(8,128)(2,1)S(1)} %all_gather.7, bf16[1024,1024]{1,0:T(8,128)(2,1)S(1)} %bitcast.68), kind=kOutput, calls=%fused_computation.6 | convolution fusion | flops 1075052544 | bytes 4718592 | tf_op jit(solution)/shard_map/dot_general | solution.py:38
  (19 shorter events, 0.8 us)
Async XLA Ops:
  6.5 80.8 %all-gather.2.cloned.1.call-start = ((), (), s32[]{:S(2)}) async-start(), calls=%async_computation.1 | async-start | bytes 4456448 | tf_op jit(solution)/shard_map/all_gather | solution.py:27
  12.1 258.1 %all-to-all-start = ((bf16[64,16,1024]{2,0,1:T(8,128)(2,1)}), bf16[64,16,1024]{2,0,1:T(8,128)(2,1)S(1)}, u32[]{:S(2)}, u32[]{:S(2)}) async-start(bf16[64,16,1024]{2,0,1:T(8,128)(2,1)} %bitcast.67), calls=%async_computation | async-start | bytes 4194304 | tf_op jit(solution)/shard_map/all_to_all | solution.py:36
  19.5 165.9 %all-reduce.3.cloned.1.call-start = ((), (), s32[]{:S(2)}) async-start(), calls=%async_computation.2 | async-start | bytes 524288 | tf_op jit(solution)/shard_map/psum | solution.py:31
Sparse Core Ops, SparseCore 0:
  9.5 77.7 all-gather.1
  93.1 92.2 all-reduce.2
where the time goes:
time: 281 us
  waiting for transfers between devices  161 us (57%)
  other arithmetic  58 us (21%)
  blocking collectives  22.3 us (8%)
  between operations  14.8 us (5%)
  matrix products  10.3 us (4%)
  starting transfers between devices  7.43 us (3%)
  local copies, waits for them, and re-layouts  6.76 us (2%)
    psum x1, waiting for transfers between devices, shards(): gram_sum = lax.psum(inner_rows(factors, factors), 'row')  92.4 us
    all_gather x1, waiting for transfers between devices, shards(): lax.all_gather(basis, 'row', axis=0, tiled=True)  67.8 us
    another operation x6, other arithmetic, shards(): chol_factor = jnp.linalg.cholesky(gram_sum)  34 us
    all_gather x1, blocking collectives, shards(): whitened = lax.all_gather(local_white, 'row', axis=0, tiled=True)  22.3 us
    another operation x4, other arithmetic, whiten_rows(): lax.linalg.triangular_solve(chol_factor, factors.astype(jnp.float32), lef...  19.7 us
    all_to_all x1, starting transfers between devices, shards(): lax.all_to_all(task_sum, 'row', split_axis=1, concat_axis=0, tiled=True)  7.39 us
  transfers between devices with their start and end apart: 3, of which 2 were waited for; matrix products, arithmetic and copies ran while one was open for 25% of the time, Pallas kernels for 0%

commit v1 on v0

--- a/solution.py
+++ b/solution.py
@@ -1,7 +1,18 @@
+import functools
+
 import jax
 import jax.numpy as jnp
 from jax import lax
+from jax.experimental import pallas as pl
+from jax.experimental.pallas import tpu as pltpu
 from jax.sharding import PartitionSpec as P
+
+MESH = pl.DeviceIdType.MESH
+F32 = jnp.float32
+BF16 = jnp.bfloat16
+EXACT = lax.Precision.HIGHEST
+PANEL = 32
+GROUP = 8
 
 
 def whiten_rows(factors, chol_factor):
@@ -16,7 +27,13 @@
     )
 
 
-def shards(deltas, basis):
+def outer_rows(left, right):
+    return lax.dot_general(
+        left, right, (((1,), (1,)), ((), ())), preferred_element_type=jnp.float32
+    )
+
+
+def general_shards(deltas, basis):
     group_deltas = deltas[0]
     task_count, rows_local, col_count = group_deltas.shape
     rank_width = basis.shape[1]
@@ -41,9 +58,399 @@
     return merged.astype(jnp.bfloat16)[None]
 
 
+def panel_inverse(block):
+    shape = block.shape
+    row = lax.broadcasted_iota(jnp.int32, shape, 0)
+    lane = lax.broadcasted_iota(jnp.int32, shape, 1)
+    work = jnp.where(lane < PANEL, block, 0.0) + jnp.where(lane == row + PANEL, 1.0, 0.0)
+    pivots = jnp.ones(shape, F32)
+    for start in range(0, PANEL, GROUP):
+        cols = [
+            jnp.broadcast_to(work[:, j : j + 1], shape) for j in range(start, start + GROUP)
+        ]
+        for at in range(GROUP):
+            j = start + at
+            pivot = cols[at][j : j + 1, :]
+            pivots = jnp.where(row == j, pivot, pivots)
+            scale = jnp.where(row > j, cols[at] * (1.0 / pivot), 0.0)
+            work = work - scale * work[j : j + 1, :]
+            for later in range(at + 1, GROUP):
+                cols[later] = cols[later] - scale * cols[later][j : j + 1, :]
+    root = lax.rsqrt(pivots)
+    root = root * (1.5 - 0.5 * pivots * root * root)
+    return (work * root)[:, PANEL : 2 * PANEL]
+
+
+def chol_inverse(aug):
+    size = aug.shape[0]
+
+    @pl.loop(0, size // PANEL)
+    def _(k):
+        at = pl.multiple_of(k * PANEL, PANEL)
+        rows = aug[pl.ds(at, PANEL), :]
+        turned = pltpu.roll(rows[:, :size], lax.rem(size - at, size), 1)
+        inverse = panel_inverse(turned[:, :128])
+        done = lax.dot_general(
+            inverse, rows, (((1,), (0,)), ((), ())), precision=EXACT, preferred_element_type=F32
+        )
+        lane = lax.broadcasted_iota(jnp.int32, (PANEL, size), 1)
+        below = jnp.where(lane >= at + PANEL, done[:, :size], 0.0)
+        aug[...] -= lax.dot_general(
+            below, done, (((0,), (0,)), ((), ())), precision=EXACT, preferred_element_type=F32
+        )
+        aug[pl.ds(at, PANEL), :] = done
+
+
+def kernel(
+    lines,
+    deltas,
+    basis,
+    white,
+    coeffs,
+    held,
+    sums,
+    columns,
+    bases,
+    factors,
+    sketch,
+    aug,
+    total,
+    load_sem,
+    basis_line,
+    basis_side,
+    basis_over,
+    basis_core,
+    basis_recv,
+    sum_send,
+    sum_recv,
+    factor_line,
+    factor_side,
+    factor_core,
+    factor_recv,
+):
+    layer = lax.axis_index("layer")
+    me = lax.axis_index("row")
+    z, y, c = me // 4, lax.rem(me // 2, 2), lax.rem(me, 2)
+    n = 4 * lines
+    depth = basis.shape[0]
+    half = depth // 2
+    tasks, rows_local, _ = held.shape
+    width = columns.shape[1]
+
+    def row_of(zz, yy, cc):
+        return (zz * 2 + yy) * 2 + cc
+
+    chunk = held.shape[2] // 4
+    loads = []
+    for i in range(4):
+        load = pltpu.make_async_copy(
+            deltas.at[:, :, pl.ds(i * chunk, chunk)],
+            held.at[:, :, pl.ds(i * chunk, chunk)],
+            load_sem.at[i],
+        )
+        load.start()
+        loads.append(load)
+
+    barrier = pltpu.get_barrier_semaphore()
+    for k in range(1, n):
+        pl.semaphore_signal(
+            barrier, inc=1, device_id=(layer, lax.rem(me + k, n)), device_id_type=MESH
+        )
+    pl.semaphore_signal(barrier, inc=1, device_id=(1 - layer, me), device_id_type=MESH)
+    bases[me] = basis[...]
+    sketch[...] = jnp.zeros_like(sketch)
+    pl.semaphore_wait(barrier, n)
+
+    sent = []
+
+    def start(copy, valid=None):
+        if valid is None:
+            copy.start()
+        else:
+            pl.when(valid)(copy.start)
+        sent.append((copy, valid))
+
+    def basis_copy(block, part, sem, to):
+        place = bases.at[block, pl.ds(pl.multiple_of(part * half, half), half), :]
+        return pltpu.make_async_remote_copy(
+            src_ref=place,
+            dst_ref=place,
+            send_sem=sem,
+            recv_sem=basis_recv.at[block, part],
+            device_id=to,
+            device_id_type=MESH,
+        )
+
+    def got_basis(block, part):
+        basis_copy(block, part, basis_core.at[block, part], (1 - layer, me)).wait_recv()
+
+    def to_side(block, valid=None):
+        start(
+            basis_copy(block, layer, basis_side.at[block], (layer, row_of(z, 1 - y, c))), valid
+        )
+
+    def to_over(block, valid=None):
+        start(basis_copy(block, layer, basis_over.at[block], (1 - layer, me)), valid)
+
+    def to_core(block, part, valid=None):
+        start(
+            basis_copy(
+                block, part, basis_core.at[block, part], (layer, row_of(z, y, 1 - c))
+            ),
+            valid,
+        )
+
+    def to_line(block, step, valid):
+        start(
+            basis_copy(block, layer, basis_line.at[block, (step + 1) // 2], (layer, row_of(z + step, y, c))),
+            valid,
+        )
+
+    def use_basis(block):
+        at = pl.multiple_of(block * depth, depth)
+        for t in range(tasks):
+            sketch[t] += jnp.dot(
+                held[t, :, pl.ds(at, depth)], bases[block], preferred_element_type=F32
+            )
+
+    def when(valid, run):
+        if valid is None:
+            run()
+        else:
+            pl.when(valid)(run)
+
+    def at_distance(d):
+        if d == 0:
+            return [(z, 0, None)]
+        return [(z - d, -1, z - d >= 0), (z + d, 1, z + d < lines)]
+
+    to_line(me, 1, z + 1 < lines)
+    to_line(me, -1, z >= 1)
+    to_side(me)
+    to_core(me, layer)
+    to_core(me, 1 - layer)
+
+    for load in loads:
+        load.wait()
+
+    def sum_copy(k):
+        to = lax.rem(me + k, n)
+        return pltpu.make_async_remote_copy(
+            src_ref=sums.at[to],
+            dst_ref=columns.at[pl.ds(pl.multiple_of(me * rows_local, rows_local), rows_local), :],
+            send_sem=sum_send.at[to],
+            recv_sem=sum_recv.at[me],
+            device_id=(layer, to),
+            device_id_type=MESH,
+        )
+
+    def got_sum(source):
+        pltpu.make_async_remote_copy(
+            src_ref=sums.at[source],
+            dst_ref=columns.at[
+                pl.ds(pl.multiple_of(source * rows_local, rows_local), rows_local), :
+            ],
+            send_sem=sum_send.at[source],
+            recv_sem=sum_recv.at[source],
+            device_id=(1 - layer, me),
+            device_id_type=MESH,
+        ).wait_recv()
+
+    def task_sum(to):
+        at = pl.ds(pl.multiple_of(to * width, width), width)
+        result = held[0, :, at].astype(F32)
+        for t in range(1, tasks):
+            result = result + held[t, :, at].astype(F32)
+        return result.astype(BF16)
+
+    @pl.loop(1, n)
+    def _(k):
+        to = lax.rem(me + k, n)
+        sums[to] = task_sum(to)
+        sum_copy(k).start()
+
+    columns[pl.ds(pl.multiple_of(me * rows_local, rows_local), rows_local), :] = task_sum(me)
+    use_basis(me)
+
+    for tick in range(lines + 3):
+        if 1 <= tick < lines:
+            for zz, step, valid in at_distance(tick):
+                block = row_of(zz, y, c)
+                when(valid, functools.partial(got_basis, block, layer))
+                onward = z + 1 < lines if step < 0 else z >= 1
+                to_line(block, -step, jnp.logical_and(valid, onward))
+                to_side(block, valid)
+                to_over(block, valid)
+                to_core(block, layer, valid)
+        if 0 <= tick - 1 < lines:
+            for zz, _, valid in at_distance(tick - 1):
+                block = row_of(zz, 1 - y, c)
+                when(valid, functools.partial(got_basis, block, layer))
+                to_over(block, valid)
+                to_core(block, layer, valid)
+        if 0 <= tick - 2 < lines:
+            for zz, _, valid in at_distance(tick - 2):
+                for yy in (y, 1 - y):
+                    if tick == 2 and yy is y:
+                        continue
+                    block = row_of(zz, yy, c)
+                    when(valid, functools.partial(got_basis, block, 1 - layer))
+                    to_core(block, 1 - layer, valid)
+                    when(valid, functools.partial(use_basis, block))
+        if 0 <= tick - 3 < lines:
+            for zz, _, valid in at_distance(tick - 3):
+                for yy in (y, 1 - y):
+                    block = row_of(zz, yy, 1 - c)
+                    when(valid, functools.partial(got_basis, block, layer))
+                    when(valid, functools.partial(got_basis, block, 1 - layer))
+                    when(valid, functools.partial(use_basis, block))
+
+    def factor_place(block):
+        return factors.at[pl.ds(pl.multiple_of(block * rows_local, rows_local), rows_local), :]
+
+    def factor_copy(block, sem, to):
+        return pltpu.make_async_remote_copy(
+            src_ref=factor_place(block),
+            dst_ref=factor_place(block),
+            send_sem=sem,
+            recv_sem=factor_recv.at[block],
+            device_id=(layer, to),
+            device_id_type=MESH,
+        )
+
+    def got_factor(block):
+        factor_copy(block, factor_core.at[block], row_of(z, y, 1 - c)).wait_recv()
+
+    own = [sketch[t].astype(BF16) for t in range(tasks)]
+    factors[pl.ds(pl.multiple_of(me * rows_local, rows_local), rows_local), :] = jnp.concatenate(
+        own, axis=1
+    )
+    for k in range(1, lines):
+        to = row_of(lax.rem(z + k, lines), y, c)
+        start(factor_copy(me, factor_line.at[k], to))
+
+    def factor_to_side(block):
+        start(factor_copy(block, factor_side.at[block], row_of(z, 1 - y, c)))
+
+    def factor_to_core(block):
+        start(factor_copy(block, factor_core.at[block], row_of(z, y, 1 - c)))
+
+    factor_to_side(me)
+    factor_to_core(me)
+    for k in range(1, lines):
+        block = row_of(lax.rem(z + k, lines), y, c)
+        got_factor(block)
+        factor_to_side(block)
+        factor_to_core(block)
+    for k in range(lines):
+        block = row_of(lax.rem(z + k, lines), 1 - y, c)
+        got_factor(block)
+        factor_to_core(block)
+    for k in range(lines):
+        for yy in (y, 1 - y):
+            got_factor(row_of(lax.rem(z + k, lines), yy, 1 - c))
+
+    size = aug.shape[0]
+    aug[:, :size] = inner_rows(factors[...], factors[...])
+    aug[:, size:] = jnp.where(
+        lax.broadcasted_iota(jnp.int32, (size, size), 0)
+        == lax.broadcasted_iota(jnp.int32, (size, size), 1),
+        1.0,
+        0.0,
+    )
+    chol_inverse(aug)
+    rest = aug[:, size:]
+    result = None
+    for _ in range(3):
+        piece = rest.astype(BF16)
+        rest = rest - piece.astype(F32)
+        term = outer_rows(factors[...], piece)
+        result = term if result is None else result + term
+    white[...] = result.astype(BF16)
+
+    group = 4 * rows_local
+    for k in range(lines):
+        zz = lax.rem(z + k, lines)
+        for yy, cc in ((y, c), (y, 1 - c), (1 - y, c), (1 - y, 1 - c)):
+            if k == 0 and yy is y and cc is c:
+                continue
+            got_sum(row_of(zz, yy, cc))
+        at = pl.ds(pl.multiple_of(zz * group, group), group)
+        term = inner_rows(white[at, :], columns[at, :])
+        if k == 0:
+            total[...] = term
+        elif k < lines - 1:
+            total[...] += term
+        else:
+            coeffs[...] = (total[...] + term).astype(BF16)
+
+    for copy, valid in sent:
+        when(valid, copy.wait_send)
+
+    @pl.loop(1, n)
+    def _(k):
+        sum_copy(k).wait_send()
+
+
+def line_shards(n, deltas, basis):
+    tasks, rows_local, cols = deltas.shape[1:]
+    depth, rank = basis.shape
+    size = tasks * rank
+    width = cols // n
+    rows = rows_local * n
+    lines = n // 4
+    dma = pltpu.SemaphoreType.DMA
+    white, coeffs = pl.pallas_call(
+        functools.partial(kernel, lines),
+        out_shape=(
+            jax.ShapeDtypeStruct((rows, size), BF16),
+            jax.ShapeDtypeStruct((size, width), BF16),
+        ),
+        in_specs=[
+            pl.BlockSpec(memory_space=pl.ANY),
+            pl.BlockSpec(memory_space=pltpu.VMEM),
+        ],
+        out_specs=[pl.BlockSpec(memory_space=pltpu.VMEM)] * 2,
+        scratch_shapes=[
+            pltpu.VMEM((tasks, rows_local, cols), BF16),
+            pltpu.VMEM((n, rows_local, width), BF16),
+            pltpu.VMEM((rows, width), BF16),
+            pltpu.VMEM((n, depth, rank), BF16),
+            pltpu.VMEM((rows, size), BF16),
+            pltpu.VMEM((tasks, rows_local, rank), F32),
+            pltpu.VMEM((size, 2 * size), F32),
+            pltpu.VMEM((size, width), F32),
+            dma((4,)),
+            dma((n, 2)),
+            dma((n,)),
+            dma((n,)),
+            dma((n, 2)),
+            dma((n, 2)),
+            dma((n,)),
+            dma((n,)),
+            dma((lines,)),
+            dma((n,)),
+            dma((n,)),
+            dma((n,)),
+        ],
+        compiler_params=pltpu.CompilerParams(
+            collective_id=0, has_side_effects=True, vmem_limit_bytes=48 * 2**20
+        ),
+        cost_estimate=pl.CostEstimate(
+            flops=4 * rows * size * width, bytes_accessed=8 * 2**20, transcendentals=0
+        ),
+    )(deltas[0], basis)
+    merged = lax.dot_general(
+        white, coeffs, (((1,), (0,)), ((), ())), preferred_element_type=F32
+    )
+    return merged.astype(BF16)[None]
+
+
 def solution(mesh):
+    n = mesh.shape["row"]
+    fits = n == 16 and mesh.shape["layer"] == 2
     return jax.shard_map(
-        shards,
+        functools.partial(line_shards, n) if fits else general_shards,
         mesh=mesh,
         in_specs=(P("layer", None, "row", None), P("row", None)),
         out_specs=P("layer", None, "row"),

time: 281 us -> 105 us (0.37)
  waiting for transfers between devices: 161 us -> 0 us
  Pallas kernels: 0 us -> 99.3 us
  other arithmetic: 58 us -> 0 us
  blocking collectives: 22.3 us -> 0 us
  between operations: 14.8 us -> 0.01 us
  matrix products: 10.3 us -> 2.03 us
  starting transfers between devices: 7.43 us -> 0 us
  local copies, waits for them, and re-layouts: 6.76 us -> 3.14 us
    pallas_call x0 -> x1, Pallas kernels: none -> 99.3 us  [line_shards(): pl.pallas_call(functools.partial(kernel, lines), out_shape=(jax.ShapeDtyp...]
    psum x1 -> x0, waiting for transfers between devices: 92.4 us -> none  [shards(): gram_sum = lax.psum(inner_rows(factors, factors), 'row')]
    all_gather x1 -> x0, waiting for transfers between devices: 67.8 us -> none  [shards(): lax.all_gather(basis, 'row', axis=0, tiled=True)]
    another operation x10 -> x0, other arithmetic: 53.7 us -> none  [the longest x6 34 us: shards(): chol_factor = jnp.linalg.cholesky(gram_sum)]
    all_gather x1 -> x0, blocking collectives: 22.3 us -> none  [shards(): whitened = lax.all_gather(local_white, 'row', axis=0, tiled=True)]
    all_to_all x1 -> x0, starting transfers between devices: 7.39 us -> none  [shards(): lax.all_to_all(task_sum, 'row', split_axis=1, concat_axis=0, tiled=True)]
    dot_general x3 -> x1, matrix products: 9.2 us -> 2.03 us  [line_shards(): lax.dot_general(white, coeffs, (((1,), (0,)), ((), ())), preferred_elemen...]
    another operation x9 -> x0, local copies, waits for them, and re-layouts: 4.12 us -> none
  transfers between devices with their start and end apart: 3 -> 0, of which waited for: 2 -> 0; matrix products, arithmetic and copies ran while one was open for 25% -> 0% of each run, Pallas kernels for 0% -> 0%
where the time goes in v1:
time: 105 us; the launch traced here: 104 us
  Pallas kernels  99.3 us (95%)
  local copies, waits for them, and re-layouts  3.14 us (3%)
  matrix products  2.03 us (2%)
    pallas_call x1, Pallas kernels, line_shards(): pl.pallas_call(functools.partial(kernel, lines), out_shape=(jax.ShapeDtyp...  99.3 us
    unnamed x4, local copies, waits for them, and re-layouts  3.14 us

profile of v1, /device:TPU:0, one launch (start us, length us, event | category | flops | bytes accessed | tf_op | source)
XLA Modules:
  0.0 104.5 jit_solution(8980617457266278373)
XLA Ops:
  0.0 0.0 copy-start
  0.0 2.2 %copy-done = bf16[1,2,64,16384]{3,2,1,0:T(8,128)(2,1)S(1)} copy-done((bf16[1,2,64,16384]{3,2,1,0:T(8,128)(2,1)S(1)}, bf16[1,2,64,16384]{3,2,1,0:T(8,128)(2,1)}, u32[]{:S(2)}) %copy-start) | copy-done | bytes 4194328
  2.2 0.0 copy-start.1
  2.2 0.9 copy-done.1
  3.1 99.3 %shard_map.28 = (bf16[1024,256]{1,0:T(8,128)(2,1)S(1)}, bf16[256,1024]{1,0:T(8,128)(2,1)S(1)}) custom-call(bf16[2,64,16384]{2,1,0:T(8,128)(2,1)S(1)} %bitcast.5, bf16[1024,128]{1,0:T(8,128)(2,1)S(1)} %copy-done.1), custom_call_target="tpu_custom_call" | custom-call | flops 1073741824 | bytes 8388608 | tf_op jit(solution)/shard_map/pallas_call | solution.py:403
  102.5 2.0 %convert_bitcast_fusion = bf16[1,1024,1024]{2,1,0:T(8,128)(2,1)} fusion(bf16[1024,256]{1,0:T(8,128)(2,1)S(1)} %get-tuple-element.7, bf16[256,1024]{1,0:T(8,128)(2,1)S(1)} %get-tuple-element.8), kind=kOutput, calls=%fused_computation | convolution fusion | flops 537919488 | bytes 3145728 | tf_op jit(solution)/shard_map/dot_general | solution.py:443
Async XLA Ops:
  0.0 2.2 %copy-start = (bf16[1,2,64,16384]{3,2,1,0:T(8,128)(2,1)S(1)}, bf16[1,2,64,16384]{3,2,1,0:T(8,128)(2,1)}, u32[]{:S(2)}) copy-start(bf16[1,2,64,16384]{3,2,1,0:T(8,128)(2,1)} %param.2) | copy-start | bytes 12582916
  2.2 0.9 copy-start.1

commit v2 on v1

--- a/solution.py
+++ b/solution.py
@@ -11,8 +11,9 @@
 F32 = jnp.float32
 BF16 = jnp.bfloat16
 EXACT = lax.Precision.HIGHEST
-PANEL = 32
-GROUP = 8
+PANEL = 64
+GROUP = 16
+PACE = (0, 1, 1, 1, 1, 1, 1, 0)
 
 
 def whiten_rows(factors, chol_factor):
@@ -83,22 +84,24 @@
 
 def chol_inverse(aug):
     size = aug.shape[0]
-
-    @pl.loop(0, size // PANEL)
-    def _(k):
-        at = pl.multiple_of(k * PANEL, PANEL)
-        rows = aug[pl.ds(at, PANEL), :]
-        turned = pltpu.roll(rows[:, :size], lax.rem(size - at, size), 1)
-        inverse = panel_inverse(turned[:, :128])
+    for at in range(0, size, PANEL):
+        after = at + PANEL
+        rows = aug[at:after, :]
+        inverse = panel_inverse(rows[:, at : at + 128] if at % 128 == 0 else pltpu.roll(
+            rows[:, at - at % 128 : at - at % 128 + 128], 128 - at % 128, 1
+        ))
         done = lax.dot_general(
             inverse, rows, (((1,), (0,)), ((), ())), precision=EXACT, preferred_element_type=F32
         )
-        lane = lax.broadcasted_iota(jnp.int32, (PANEL, size), 1)
-        below = jnp.where(lane >= at + PANEL, done[:, :size], 0.0)
-        aug[...] -= lax.dot_general(
-            below, done, (((0,), (0,)), ((), ())), precision=EXACT, preferred_element_type=F32
-        )
-        aug[pl.ds(at, PANEL), :] = done
+        if after < size:
+            aug[after:, :] -= lax.dot_general(
+                done[:, after:size],
+                done,
+                (((0,), (0,)), ((), ())),
+                precision=EXACT,
+                preferred_element_type=F32,
+            )
+        aug[at:after, :] = done
 
 
 def kernel(
@@ -151,14 +154,17 @@
         load.start()
         loads.append(load)
 
+    own_basis = pltpu.make_async_copy(basis, bases.at[me], load_sem.at[4])
+    own_basis.start()
+
     barrier = pltpu.get_barrier_semaphore()
     for k in range(1, n):
         pl.semaphore_signal(
             barrier, inc=1, device_id=(layer, lax.rem(me + k, n)), device_id_type=MESH
         )
     pl.semaphore_signal(barrier, inc=1, device_id=(1 - layer, me), device_id_type=MESH)
-    bases[me] = basis[...]
     sketch[...] = jnp.zeros_like(sketch)
+    own_basis.wait()
     pl.semaphore_wait(barrier, n)
 
     sent = []
@@ -184,9 +190,12 @@
     def got_basis(block, part):
         basis_copy(block, part, basis_core.at[block, part], (1 - layer, me)).wait_recv()
 
-    def to_side(block, valid=None):
+    def to_side(block, part, valid=None):
         start(
-            basis_copy(block, layer, basis_side.at[block], (layer, row_of(z, 1 - y, c))), valid
+            basis_copy(
+                block, part, basis_side.at[block, part], (layer, row_of(z, 1 - y, c))
+            ),
+            valid,
         )
 
     def to_over(block, valid=None):
@@ -208,10 +217,8 @@
 
     def use_basis(block):
         at = pl.multiple_of(block * depth, depth)
-        for t in range(tasks):
-            sketch[t] += jnp.dot(
-                held[t, :, pl.ds(at, depth)], bases[block], preferred_element_type=F32
-            )
+        left = held[:, :, pl.ds(at, depth)].reshape(tasks * rows_local, depth)
+        sketch[...] += jnp.dot(left, bases[block], preferred_element_type=F32).reshape(sketch.shape)
 
     def when(valid, run):
         if valid is None:
@@ -226,15 +233,12 @@
 
     to_line(me, 1, z + 1 < lines)
     to_line(me, -1, z >= 1)
-    to_side(me)
+    to_side(me, layer)
+    to_side(me, 1 - layer)
     to_core(me, layer)
     to_core(me, 1 - layer)
 
-    for load in loads:
-        load.wait()
-
-    def sum_copy(k):
-        to = lax.rem(me + k, n)
+    def sum_copy(to):
         return pltpu.make_async_remote_copy(
             src_ref=sums.at[to],
             dst_ref=columns.at[pl.ds(pl.multiple_of(me * rows_local, rows_local), rows_local), :],
@@ -263,47 +267,69 @@
             result = result + held[t, :, at].astype(F32)
         return result.astype(BF16)
 
-    @pl.loop(1, n)
-    def _(k):
-        to = lax.rem(me + k, n)
-        sums[to] = task_sum(to)
-        sum_copy(k).start()
-
+    corners = ((y, c), (y, 1 - c), (1 - y, c), (1 - y, 1 - c))
+    crossing = [
+        row_of(zz, yy, cc)
+        for yy, cc in corners
+        for zz in (lax.rem(z + lines // 2, lines), lines - 1 - z)
+    ]
+    staying = [row_of(z + 1 - 2 * lax.rem(z, 2), yy, cc) for yy, cc in corners]
+    staying += [row_of(z, yy, cc) for yy, cc in corners[1:]]
+    queue = crossing + staying
+    sum_copies = []
+
+    def send_sums(count):
+        for _ in range(min(count, len(queue))):
+            to = queue.pop(0)
+            sums[to] = task_sum(to)
+            copy = sum_copy(to)
+            copy.start()
+            sum_copies.append(copy)
+
+    for load in loads:
+        load.wait()
     columns[pl.ds(pl.multiple_of(me * rows_local, rows_local), rows_local), :] = task_sum(me)
     use_basis(me)
 
     for tick in range(lines + 3):
+        ready = []
         if 1 <= tick < lines:
             for zz, step, valid in at_distance(tick):
                 block = row_of(zz, y, c)
                 when(valid, functools.partial(got_basis, block, layer))
                 onward = z + 1 < lines if step < 0 else z >= 1
                 to_line(block, -step, jnp.logical_and(valid, onward))
-                to_side(block, valid)
+                to_side(block, layer, valid)
                 to_over(block, valid)
                 to_core(block, layer, valid)
         if 0 <= tick - 1 < lines:
             for zz, _, valid in at_distance(tick - 1):
                 block = row_of(zz, 1 - y, c)
                 when(valid, functools.partial(got_basis, block, layer))
-                to_over(block, valid)
                 to_core(block, layer, valid)
-        if 0 <= tick - 2 < lines:
+                if tick == 1:
+                    got_basis(block, 1 - layer)
+                    to_core(block, 1 - layer)
+                    ready.append((block, None))
+                else:
+                    to_over(block, valid)
+        if 1 <= tick - 2 < lines:
             for zz, _, valid in at_distance(tick - 2):
                 for yy in (y, 1 - y):
-                    if tick == 2 and yy is y:
-                        continue
                     block = row_of(zz, yy, c)
                     when(valid, functools.partial(got_basis, block, 1 - layer))
                     to_core(block, 1 - layer, valid)
-                    when(valid, functools.partial(use_basis, block))
+                    ready.append((block, valid))
         if 0 <= tick - 3 < lines:
             for zz, _, valid in at_distance(tick - 3):
                 for yy in (y, 1 - y):
                     block = row_of(zz, yy, 1 - c)
                     when(valid, functools.partial(got_basis, block, layer))
                     when(valid, functools.partial(got_basis, block, 1 - layer))
-                    when(valid, functools.partial(use_basis, block))
+                    ready.append((block, valid))
+        send_sums(PACE[tick])
+        for block, valid in ready:
+            when(valid, functools.partial(use_basis, block))
 
     def factor_place(block):
         return factors.at[pl.ds(pl.multiple_of(block * rows_local, rows_local), rows_local), :]
@@ -337,6 +363,7 @@
 
     factor_to_side(me)
     factor_to_core(me)
+    send_sums(PACE[lines + 3])
     for k in range(1, lines):
         block = row_of(lax.rem(z + k, lines), y, c)
         got_factor(block)
@@ -349,6 +376,8 @@
     for k in range(lines):
         for yy in (y, 1 - y):
             got_factor(row_of(lax.rem(z + k, lines), yy, 1 - c))
+
+    send_sums(len(queue))
 
     size = aug.shape[0]
     aug[:, :size] = inner_rows(factors[...], factors[...])
@@ -387,9 +416,8 @@
     for copy, valid in sent:
         when(valid, copy.wait_send)
 
-    @pl.loop(1, n)
-    def _(k):
-        sum_copy(k).wait_send()
+    for copy in sum_copies:
+        copy.wait_send()
 
 
 def line_shards(n, deltas, basis):
@@ -406,10 +434,7 @@
             jax.ShapeDtypeStruct((rows, size), BF16),
             jax.ShapeDtypeStruct((size, width), BF16),
         ),
-        in_specs=[
-            pl.BlockSpec(memory_space=pl.ANY),
-            pl.BlockSpec(memory_space=pltpu.VMEM),
-        ],
+        in_specs=[pl.BlockSpec(memory_space=pl.ANY)] * 2,
         out_specs=[pl.BlockSpec(memory_space=pltpu.VMEM)] * 2,
         scratch_shapes=[
             pltpu.VMEM((tasks, rows_local, cols), BF16),
@@ -420,13 +445,13 @@
             pltpu.VMEM((tasks, rows_local, rank), F32),
             pltpu.VMEM((size, 2 * size), F32),
             pltpu.VMEM((size, width), F32),
-            dma((4,)),
-            dma((n, 2)),
-            dma((n,)),
-            dma((n,)),
+            dma((5,)),
             dma((n, 2)),
             dma((n, 2)),
             dma((n,)),
+            dma((n, 2)),
+            dma((n, 2)),
+            dma((n,)),
             dma((n,)),
             dma((lines,)),
             dma((n,)),
@@ -434,7 +459,7 @@
             dma((n,)),
         ],
         compiler_params=pltpu.CompilerParams(
-            collective_id=0, has_side_effects=True, vmem_limit_bytes=48 * 2**20
+            collective_id=0, has_side_effects=True, vmem_limit_bytes=60 * 2**20
         ),
         cost_estimate=pl.CostEstimate(
             flops=4 * rows * size * width, bytes_accessed=8 * 2**20, transcendentals=0

time: 105 us -> 82.2 us (0.78)
  Pallas kernels: 99.3 us -> 78.8 us
  local copies, waits for them, and re-layouts: 3.14 us -> 0 us
  matrix products: 2.03 us -> 3.23 us
    pallas_call x1, Pallas kernels: 99.3 us -> 78.8 us  [line_shards(): pl.pallas_call(functools.partial(kernel, lines), out_shape=(jax.ShapeDtyp...]
    unnamed x4 -> x0, local copies, waits for them, and re-layouts: 3.14 us -> none
    dot_general x1, matrix products: 2.03 us -> 3.23 us  [line_shards(): lax.dot_general(white, coeffs, (((1,), (0,)), ((), ())), preferred_elemen...]
where the time goes in v2:
time: 82.2 us; the launch traced here: 82.1 us
  Pallas kernels  78.8 us (96%)
  matrix products  3.23 us (4%)
    pallas_call x1, Pallas kernels, line_shards(): pl.pallas_call(functools.partial(kernel, lines), out_shape=(jax.ShapeDtyp...  78.8 us
    dot_general x1, matrix products, line_shards(): lax.dot_general(white, coeffs, (((1,), (0,)), ((), ())), preferred_elemen...  3.23 us

profile of v2, /device:TPU:0, one launch (start us, length us, event | category | flops | bytes accessed | tf_op | source)
XLA Modules:
  0.0 82.1 jit_solution(9302509738118537741)
XLA Ops:
  0.0 78.8 %shard_map.28 = (bf16[1024,256]{1,0:T(8,128)(2,1)}, bf16[256,1024]{1,0:T(8,128)(2,1)}) custom-call(bf16[2,64,16384]{2,1,0:T(8,128)(2,1)} %bitcast.5, bf16[1024,128]{1,0:T(8,128)(2,1)} %basis.1), custom_call_target="tpu_custom_call" | custom-call | flops 1073741824 | bytes 8388608 | tf_op jit(solution)/shard_map/pallas_call | solution.py:431
  78.8 3.2 %convert_bitcast_fusion = bf16[1,1024,1024]{2,1,0:T(8,128)(2,1)} fusion(bf16[1024,256]{1,0:T(8,128)(2,1)} %get-tuple-element.7, bf16[256,1024]{1,0:T(8,128)(2,1)} %get-tuple-element.8), kind=kOutput, calls=%fused_computation | convolution fusion | flops 537919488 | bytes 3145728 | tf_op jit(solution)/shard_map/dot_general | solution.py:468

commit v3 on v2

--- a/solution.py
+++ b/solution.py
@@ -13,7 +13,7 @@
 EXACT = lax.Precision.HIGHEST
 PANEL = 64
 GROUP = 16
-PACE = (0, 1, 1, 1, 1, 1, 1, 0)
+PACE = (0, 1, 1, 1, 0, 0, 0, 5)
 
 
 def whiten_rows(factors, chol_factor):

time: 82.2 us -> 75 us (0.912); the launches traced: 82.1 us -> 74 us
  Pallas kernels: 78.8 us -> 70.8 us
    pallas_call x1, Pallas kernels: 78.8 us -> 70.8 us  [line_shards(): pl.pallas_call(functools.partial(kernel, lines), out_shape=(jax.ShapeDtyp...]
where the time goes in v3:
time: 75 us; the launch traced here: 74 us
  Pallas kernels  70.8 us (94%)
  matrix products  3.23 us (4%)
    pallas_call x1, Pallas kernels, line_shards(): pl.pallas_call(functools.partial(kernel, lines), out_shape=(jax.ShapeDtyp...  70.8 us
    dot_general x1, matrix products, line_shards(): lax.dot_general(white, coeffs, (((1,), (0,)), ((), ())), preferred_elemen...  3.23 us

profile of v3, /device:TPU:0, one launch (start us, length us, event | category | flops | bytes accessed | tf_op | source)
XLA Modules:
  0.0 74.0 jit_solution(4828584835181829089)
XLA Ops:
  0.0 70.8 %shard_map.28 = (bf16[1024,256]{1,0:T(8,128)(2,1)}, bf16[256,1024]{1,0:T(8,128)(2,1)}) custom-call(bf16[2,64,16384]{2,1,0:T(8,128)(2,1)} %bitcast.5, bf16[1024,128]{1,0:T(8,128)(2,1)} %basis.1), custom_call_target="tpu_custom_call" | custom-call | flops 1073741824 | bytes 8388608 | tf_op jit(solution)/shard_map/pallas_call | solution.py:431
  70.8 3.2 %convert_bitcast_fusion = bf16[1,1024,1024]{2,1,0:T(8,128)(2,1)} fusion(bf16[1024,256]{1,0:T(8,128)(2,1)} %get-tuple-element.7, bf16[256,1024]{1,0:T(8,128)(2,1)} %get-tuple-element.8), kind=kOutput, calls=%fused_computation | convolution fusion | flops 537919488 | bytes 3145728 | tf_op jit(solution)/shard_map/dot_general | solution.py:468
